TPU v7x, 32 devices: a whole 2x2x4 slice. The times are simulated.
32 devices in a mesh: groups: 2 (over y), seq: 8 (over z, x), head: 1, sub: 2 (over core).
Axes of the slice: x: 2, y: 2, z: 4, core: 2. Of those that a mesh axis runs over, the one named last changes fastest.
Arguments:
- queries: bfloat16 [8, 32768, 512], P('head', ('groups', 'seq', 'sub')), parts along dimension 1, may hold values from -6 to 6
- keys: bfloat16 [8, 32768, 512], P('head', ('groups', 'seq', 'sub')), parts along dimension 1, may hold values from -6 to 6
- values: bfloat16 [8, 32768, 512], P('head', ('groups', 'seq', 'sub')), parts along dimension 1, may hold values from -6 to 6
- lr_codes: int32 [8, 32768], P('head', ('groups', 'seq', 'sub')), parts along dimension 1, may hold values from 0 to 15
- fast_gate: float32 [8, 512, 512], P('head', ('seq', 'sub')), may hold values from -0.25 to 0.25
- fast_up: float32 [8, 512, 512], P('head', ('seq', 'sub')), may hold values from -0.25 to 0.25
- fast_down: float32 [8, 512, 512], P('head', ('seq', 'sub')), may hold values from -0.25 to 0.25
Outputs:
- fast_out: bfloat16 [8, 32768, 512], P('head', ('groups', 'seq', 'sub')), parts along dimension 1
There are 2 independent parts, one for each index of `groups`. A program takes and returns all parts, laid end to end along the dimension named above; an argument that names none is the same for every part. Nothing has to cross between parts.
All inputs are finite; a program needn't handle non-finite values.
Results may differ from a plain program's by a relative error of at most 0.0085.
Values may be sent and summed in bfloat16 or wider, within the bound.
A program may use at most 192 MiB of HBM per device.

v0:
```python
import jax
import jax.numpy as jnp
from jax import lax
from jax.sharding import PartitionSpec as P

EPSILON = 1e-06
STEP_SIZE = 0.5


def column_squares(matrix):
    return jnp.sum(matrix * matrix, axis=1)


def rescale(moved, col_weight, col_moved):
    return moved * jnp.sqrt((col_weight + EPSILON) / (col_moved + EPSILON))[:, None, :]


def step_scale(col_weight, grad_total):
    return (
        STEP_SIZE * jnp.sqrt(jnp.sum(col_weight, axis=1) + EPSILON) / jnp.sqrt(grad_total + EPSILON)
    )


def apply_fast(queries, gate_b, up_b, down_b):
    query_gate = jnp.einsum("htd,hdf->htf", queries, gate_b, preferred_element_type=jnp.float32)
    query_up = jnp.einsum("htd,hdf->htf", queries, up_b, preferred_element_type=jnp.float32)
    query_hidden = (jax.nn.silu(query_gate) * query_up).astype(jnp.bfloat16)
    return jnp.einsum(
        "htf,hfd->htd", query_hidden, down_b, preferred_element_type=jnp.float32
    ).astype(jnp.bfloat16)


def local_grads(keys, target, gate_b, up_b, down_b):
    gate_pre = jnp.einsum("htd,hdf->htf", keys, gate_b, preferred_element_type=jnp.float32)
    up_pre = jnp.einsum("htd,hdf->htf", keys, up_b, preferred_element_type=jnp.float32)
    sigmoid_gate = jax.nn.sigmoid(gate_pre)
    hidden = (gate_pre * sigmoid_gate * up_pre).astype(jnp.bfloat16)
    back = jnp.einsum("htd,hfd->htf", target, down_b, preferred_element_type=jnp.float32)
    grad_gate_pre = (back * up_pre * sigmoid_gate * (1.0 + gate_pre * (1.0 - sigmoid_gate))).astype(
        jnp.bfloat16
    )
    grad_up_pre = (back * gate_pre * sigmoid_gate).astype(jnp.bfloat16)
    grad_gate = jnp.einsum("htd,htf->hdf", keys, grad_gate_pre, preferred_element_type=jnp.float32)
    grad_up = jnp.einsum("htd,htf->hdf", keys, grad_up_pre, preferred_element_type=jnp.float32)
    grad_down = jnp.einsum("htf,htd->hfd", hidden, target, preferred_element_type=jnp.float32)
    return (grad_gate, grad_up, grad_down)


def on_device(queries, keys, values, lr_codes, fast_gate, fast_up, fast_down):
    token_rates = (lr_codes.astype(jnp.float32) + 1.0) / 16.0
    target = (-token_rates[:, :, None] * values.astype(jnp.float32)).astype(jnp.bfloat16)
    gate_b, up_b, down_b = (
        lax.all_gather(fast_gate.astype(jnp.bfloat16), ("seq", "sub"), axis=1, tiled=True),
        lax.all_gather(fast_up.astype(jnp.bfloat16), ("seq", "sub"), axis=1, tiled=True),
        lax.all_gather(fast_down.astype(jnp.bfloat16), ("seq", "sub"), axis=1, tiled=True),
    )
    grad_gate, grad_up, grad_down = local_grads(keys, target, gate_b, up_b, down_b)
    owned = (
        lax.psum_scatter(grad_gate, ("seq", "sub"), scatter_dimension=1, tiled=True),
        lax.psum_scatter(grad_up, ("seq", "sub"), scatter_dimension=1, tiled=True),
        lax.psum_scatter(grad_down, ("seq", "sub"), scatter_dimension=1, tiled=True),
    )
    weights = (fast_gate, fast_up, fast_down)
    grad_local = jnp.stack(
        [
            jnp.sum(owned[0] * owned[0], axis=(1, 2)),
            jnp.sum(owned[1] * owned[1], axis=(1, 2)),
            jnp.sum(owned[2] * owned[2], axis=(1, 2)),
        ],
        axis=1,
    )
    col_gate, col_up, col_down, grad_totals = lax.psum(
        (column_squares(fast_gate), column_squares(fast_up), column_squares(fast_down), grad_local),
        ("seq", "sub"),
    )
    col_weights = (col_gate, col_up, col_down)
    moved_all = []
    for index in range(3):
        scale = step_scale(col_weights[index], grad_totals[:, index])
        moved_all.append(weights[index] - scale[:, None, None] * owned[index])
    moved_cols = lax.psum(
        (column_squares(moved_all[0]), column_squares(moved_all[1]), column_squares(moved_all[2])),
        ("seq", "sub"),
    )
    renewed = [
        rescale(moved_all[index], col_weights[index], moved_cols[index]).astype(jnp.bfloat16)
        for index in range(3)
    ]
    new_gate, new_up, new_down = (
        lax.all_gather(renewed[0], ("seq", "sub"), axis=1, tiled=True),
        lax.all_gather(renewed[1], ("seq", "sub"), axis=1, tiled=True),
        lax.all_gather(renewed[2], ("seq", "sub"), axis=1, tiled=True),
    )
    return apply_fast(queries, new_gate, new_up, new_down)


def solution(mesh):
    return jax.shard_map(
        on_device,
        mesh=mesh,
        in_specs=(
            P("head", ("groups", "seq", "sub"), None),
            P("head", ("groups", "seq", "sub"), None),
            P("head", ("groups", "seq", "sub"), None),
            P("head", ("groups", "seq", "sub")),
            P("head", ("seq", "sub"), None),
            P("head", ("seq", "sub"), None),
            P("head", ("seq", "sub"), None),
        ),
        out_specs=P("head", ("groups", "seq", "sub"), None),
        check_vma=False,
    )
```

profile of v0, /device:TPU:0, one launch (start us, length us, event | category | flops | bytes accessed | tf_op | source)
XLA Modules:
  0.0 794.0 jit_solution(1773407533182401554)
XLA Ops:
  6.5 0.0 all-gather.11.cloned.1.call-start
  6.5 2.6 multiply_reduce_fusion.8
  9.1 0.0 all-gather.11.cloned.1.call-update
  9.1 0.0 all-gather.7.cloned.1.call-start
  9.2 2.6 multiply_reduce_fusion.1
  11.8 0.0 all-gather.7.cloned.1.call-update
  11.8 0.0 all-gather.9.cloned.1.call-start
  11.8 2.6 multiply_reduce_fusion.3
  14.5 0.0 all-gather.9.cloned.1.call-update
  14.5 0.0 reduce-scatter.6.cloned.1.call-start
  14.6 0.8 multiply_negate_fusion
  15.3 47.5 %all-gather.11.cloned.1.call-done = bf16[8,512,512]{2,1,0:T(8,128)(2,1)} async-done(((bf16[8,32,512]{2,1,0:T(8,128)(2,1)}), bf16[8,512,512]{2,1,0:T(8,128)(2,1)}) %all-gather.11.cloned.1.call-update) | async-done | bytes 4194320 | tf_op jit(solution)/shard_map/all_gather | solution.py:53
  62.9 14.8 %fusion.19 = f32[8,1024,512]{2,1,0:T(8,128)} fusion(bf16[8,1024,512]{2,1,0:T(8,128)(2,1)} %param.8, bf16[8,512,512]{2,1,0:T(8,128)(2,1)} %all-gather.11.cloned.1.call-done), kind=kOutput, calls=%fused_computation.50 | convolution fusion | flops 4294967296 | bytes 29360128 | tf_op jit(solution)/shard_map/htd,hdf->htf/dot_general | solution.py:34
  77.7 36.5 %all-gather.7.cloned.1.call-done = bf16[8,512,512]{2,1,0:T(8,128)(2,1)} async-done(((bf16[8,32,512]{2,1,0:T(8,128)(2,1)}), bf16[8,512,512]{2,1,0:T(8,128)(2,1)}) %all-gather.7.cloned.1.call-update) | async-done | bytes 4194320 | tf_op jit(solution)/shard_map/all_gather | solution.py:55
  114.1 11.7 %fusion.7 = f32[8,1024,512]{2,1,0:T(8,128)} fusion(bf16[8,512,512]{2,1,0:T(8,128)(2,1)} %all-gather.7.cloned.1.call-done, bf16[8,1024,512]{2,1,0:T(8,128)(2,1)} %param.9, f32[8,1024]{1,0:T(8,128)S(1)} %multiply_negate_fusion), kind=kOutput, calls=%fused_computation.15 | convolution fusion | flops 4307550208 | bytes 29392896 | tf_op jit(solution)/shard_map/htd,hfd->htf/dot_general | solution.py:38
  125.8 19.5 %fusion.13 = f32[8,512,512]{1,2,0:T(8,128)} fusion(bf16[8,1024,512]{2,1,0:T(8,128)(2,1)} %param.8, f32[8,1024,512]{2,1,0:T(8,128)} %fusion.7, f32[8,1024,512]{2,1,0:T(8,128)} %fusion.19), kind=kOutput, calls=%fused_computation.21 | convolution fusion | flops 4320133120 | bytes 50331648 | tf_op jit(solution)/shard_map/htd,htf->hdf/dot_general | solution.py:44
  145.3 10.5 %copy.18 = f32[8,512,512]{2,0,1:T(8,128)} copy(f32[8,512,512]{1,2,0:T(8,128)} %fusion.13) | data formatting | bytes 16777216 | tf_op jit(solution)/shard_map/htd,htf->hdf/dot_general | solution.py:44
  155.8 0.0 reduce-scatter.6.cloned.1.call-update
  155.8 0.2 reduce-scatter.8.cloned.1.call-start
  156.0 9.4 %all-gather.9.cloned.1.call-done = bf16[8,512,512]{2,1,0:T(8,128)(2,1)} async-done(((bf16[8,32,512]{2,1,0:T(8,128)(2,1)}), bf16[8,512,512]{2,1,0:T(8,128)(2,1)}) %all-gather.9.cloned.1.call-update) | async-done | bytes 4194320 | tf_op jit(solution)/shard_map/all_gather | solution.py:54
  165.4 16.6 %fusion.18 = f32[8,1024,512]{2,1,0:T(8,128)} fusion(bf16[8,1024,512]{2,1,0:T(8,128)(2,1)} %param.8, bf16[8,512,512]{2,1,0:T(8,128)(2,1)} %all-gather.9.cloned.1.call-done), kind=kOutput, calls=%fused_computation.49 | convolution fusion | flops 4294967296 | bytes 29360128 | tf_op jit(solution)/shard_map/htd,hdf->htf/dot_general | solution.py:35
  182.0 21.8 %fusion.5 = f32[8,512,512]{2,1,0:T(8,128)} fusion(f32[8,1024,512]{2,1,0:T(8,128)} %fusion.18, f32[8,1024,512]{2,1,0:T(8,128)} %fusion.19, bf16[8,1024,512]{2,1,0:T(8,128)(2,1)} %param.9, f32[8,1024]{1,0:T(8,128)S(1)} %multiply_negate_fusion), kind=kOutput, calls=%fused_computation.13 | convolution fusion | flops 4332716032 | bytes 50364416 | tf_op jit(solution)/shard_map/htf,htd->hfd/dot_general | solution.py:45
  203.8 0.0 reduce-scatter.8.cloned.1.call-update
  203.8 0.0 reduce-scatter.4.cloned.1.call-start
  203.9 25.5 %fusion.12 = f32[8,512,512]{1,2,0:T(8,128)} fusion(bf16[8,1024,512]{2,1,0:T(8,128)(2,1)} %param.8, f32[8,1024,512]{2,1,0:T(8,128)} %fusion.19, f32[8,1024,512]{2,1,0:T(8,128)} %fusion.7, f32[8,1024,512]{2,1,0:T(8,128)} %fusion.18), kind=kOutput, calls=%fused_computation.20 | convolution fusion | flops 4336910336 | bytes 67108864 | tf_op jit(solution)/shard_map/htd,htf->hdf/dot_general | solution.py:43
  229.4 10.6 %copy.16 = f32[8,512,512]{2,0,1:T(8,128)} copy(f32[8,512,512]{1,2,0:T(8,128)} %fusion.12) | data formatting | bytes 16777216 | tf_op jit(solution)/shard_map/htd,htf->hdf/dot_general | solution.py:43
  240.0 0.0 copy-start.4
  240.0 0.0 copy-start.1
  240.0 0.0 copy-start.2
  240.0 0.0 reduce-scatter.4.cloned.1.call-update
  240.0 0.0 all-gather.13.cloned.1.call-start
  240.1 32.5 %reduce-scatter.6.cloned.1.call-done = f32[8,32,512]{2,0,1:T(8,128)} async-done(((f32[8,512,512]{2,0,1:T(8,128)}), f32[8,32,512]{2,0,1:T(8,128)}) %reduce-scatter.6.cloned.1.call-update) | async-done | bytes 524304 | tf_op jit(solution)/shard_map/reduce_scatter | solution.py:60
  272.6 1.4 multiply_reduce_fusion.6
  273.9 107.0 %reduce-scatter.8.cloned.1.call-done = f32[8,32,512]{2,1,0:T(8,128)} async-done(((f32[8,512,512]{2,1,0:T(8,128)}), f32[8,32,512]{2,1,0:T(8,128)}) %reduce-scatter.8.cloned.1.call-update) | async-done | bytes 524304 | tf_op jit(solution)/shard_map/reduce_scatter | solution.py:61
  381.0 1.2 multiply_reduce_fusion.5
  382.2 107.2 %reduce-scatter.4.cloned.1.call-done = f32[8,32,512]{2,0,1:T(8,128)} async-done(((f32[8,512,512]{2,0,1:T(8,128)}), f32[8,32,512]{2,0,1:T(8,128)}) %reduce-scatter.4.cloned.1.call-update) | async-done | bytes 524304 | tf_op jit(solution)/shard_map/reduce_scatter | solution.py:59
  489.3 1.3 multiply_reduce_fusion.7
  490.6 0.0 copy-done.4
  490.6 0.0 copy-done.5
  490.6 0.0 copy-done.6
  490.7 60.4 %all-reduce.1 = (f32[8,3]{0,1:T(4,128)S(1)}, f32[8,512]{1,0:T(8,128)S(1)}, f32[8,512]{1,0:T(8,128)S(1)}, f32[8,512]{1,0:T(8,128)S(1)}) all-reduce(f32[8,3]{0,1:T(4,128)S(1)} %pad_maximum_fusion, f32[8,512]{1,0:T(8,128)S(1)} %copy-done.5, ...), channel_id=1, replica_groups=mesh['groups'=2,'seq'=8,'head'=1,'sub'=2] {'seq','sub'}, use_global_device_ids=true, to_apply=%region_9.0 | all-reduce | flops 12312 | bytes 98496 | tf_op jit(solution)/shard_map/psum | solution.py:72
  551.0 0.1 reduce_sum.118
  551.2 0.1 reduce_sum.109
  551.3 0.1 reduce_sum.115
  551.4 0.0 copy-done
  551.4 1.2 multiply_reduce_fusion
  552.6 0.0 copy-done.1
  552.6 0.0 copy-done.2
  552.7 1.9 multiply_reduce_fusion.2
  554.6 57.7 %all-reduce = (f32[8,512]{1,0:T(8,128)S(1)}, f32[8,512]{1,0:T(8,128)S(1)}, f32[8,512]{1,0:T(8,128)S(1)}) all-reduce(f32[8,512]{1,0:T(8,128)S(1)} %multiply_reduce_fusion, f32[8,512]{1,0:T(8,128)S(1)} %get-tuple-element.22, f32[8,512]{1,0:T(8,128)S(1)} %get-tuple-element.21), channel_id=1, replica_groups=mesh['groups'=2,'seq'=8,'head'=1,'sub'=2] {'seq','sub'}, use_global_device_ids=true, to_apply=%region_21.0 | all-reduce | flops 12288 | bytes 98304 | tf_op jit(solution)/shard_map/psum | solution.py:81
  612.3 2.1 multiply_convert_fusion.15
  614.4 0.0 all-gather.13.cloned.1.call-update
  614.4 0.0 all-gather.17.cloned.1.call-start
  614.5 1.9 multiply_convert_fusion.13
  616.4 0.0 all-gather.17.cloned.1.call-update
  616.4 0.3 all-gather.15.cloned.1.call-start
  616.7 0.0 copy-done.3
  616.7 1.0 multiply_convert_fusion.14
  617.7 0.0 all-gather.15.cloned.1.call-update
  617.7 44.6 %all-gather.13.cloned.1.call-done = bf16[8,512,512]{2,0,1:T(8,128)(2,1)} async-done(((bf16[8,32,512]{2,0,1:T(8,128)(2,1)}), bf16[8,512,512]{2,0,1:T(8,128)(2,1)}) %all-gather.13.cloned.1.call-update) | async-done | bytes 4194320 | tf_op jit(solution)/shard_map/all_gather | solution.py:90
  662.3 14.9 %fusion.10 = f32[8,512,1024]{1,2,0:T(8,128)} fusion(bf16[8,1024,512]{2,1,0:T(8,128)(2,1)} %param.7, bf16[8,512,512]{2,0,1:T(8,128)(2,1)} %all-gather.13.cloned.1.call-done), kind=kOutput, calls=%fused_computation.18 | convolution fusion | flops 4294967296 | bytes 29360128 | tf_op jit(solution)/shard_map/htd,hdf->htf/dot_general | solution.py:25
  677.3 36.4 %all-gather.17.cloned.1.call-done = bf16[8,512,512]{2,1,0:T(8,128)(2,1)} async-done(((bf16[8,32,512]{2,1,0:T(8,128)(2,1)}), bf16[8,512,512]{2,1,0:T(8,128)(2,1)}) %all-gather.17.cloned.1.call-update) | async-done | bytes 4194320 | tf_op jit(solution)/shard_map/all_gather | solution.py:92
  713.6 51.2 %all-gather.15.cloned.1.call-done = bf16[8,512,512]{2,0,1:T(8,128)(2,1)} async-done(((bf16[8,32,512]{2,0,1:T(8,128)(2,1)}), bf16[8,512,512]{2,0,1:T(8,128)(2,1)}) %all-gather.15.cloned.1.call-update) | async-done | bytes 4194320 | tf_op jit(solution)/shard_map/all_gather | solution.py:91
  764.9 22.5 %convolution_convert_fusion = bf16[8,1024,512]{2,1,0:T(8,128)(2,1)} fusion(bf16[8,512,512]{2,1,0:T(8,128)(2,1)} %all-gather.17.cloned.1.call-done, f32[8,512,1024]{1,2,0:T(8,128)} %fusion.10, bf16[8,1024,512]{2,1,0:T(8,128)(2,1)} %param.7, bf16[8,512,512]{2,0,1:T(8,128)(2,1)} %all-gather.15.cloned.1.call-done), kind=kOutput, calls=%fused_computation.16 | convolution fusion | flops 8619294720 | bytes 41943040 | tf_op jit(solution)/shard_map/htf,hfd->htd/dot_general | solution.py:28
  (9 shorter events, 0.1 us)
Async XLA Ops:
  6.5 56.3 %all-gather.11.cloned.1.call-start = ((), (), s32[]{:S(2)}) async-start(), calls=%async_computation.5 | async-start | bytes 4456448 | tf_op jit(solution)/shard_map/all_gather | solution.py:53
  9.1 105.0 %all-gather.7.cloned.1.call-start = ((), (), s32[]{:S(2)}) async-start(), calls=%async_computation.3 | async-start | bytes 4456448 | tf_op jit(solution)/shard_map/all_gather | solution.py:55
  11.8 153.7 %all-gather.9.cloned.1.call-start = ((), (), s32[]{:S(2)}) async-start(), calls=%async_computation.4 | async-start | bytes 4456448 | tf_op jit(solution)/shard_map/all_gather | solution.py:54
  14.5 258.1 %reduce-scatter.6.cloned.1.call-start = ((), (), s32[]{:S(2)}) async-start(), calls=%async_computation.7 | async-start | bytes 8912896 | tf_op jit(solution)/shard_map/reduce_scatter | solution.py:60
  155.8 225.2 %reduce-scatter.8.cloned.1.call-start = ((), (), s32[]{:S(2)}) async-start(), calls=%async_computation.8 | async-start | bytes 8912896 | tf_op jit(solution)/shard_map/reduce_scatter | solution.py:61
  203.8 285.5 %reduce-scatter.4.cloned.1.call-start = ((), (), s32[]{:S(2)}) async-start(), calls=%async_computation.6 | async-start | bytes 8912896 | tf_op jit(solution)/shard_map/reduce_scatter | solution.py:59
  240.0 250.7 %copy-start.4 = (f32[8,512]{1,0:T(8,128)S(1)}, f32[8,512]{1,0:T(8,128)}, u32[]{:S(2)}) copy-start(f32[8,512]{1,0:T(8,128)} %get-tuple-element.14) | copy-start | bytes 49156
  240.0 250.7 %copy-start.5 = (f32[8,512]{1,0:T(8,128)S(1)}, f32[8,512]{1,0:T(8,128)}, u32[]{:S(2)}) copy-start(f32[8,512]{1,0:T(8,128)} %get-tuple-element.16) | copy-start | bytes 49156
  240.0 250.7 %copy-start.6 = (f32[8,512]{1,0:T(8,128)S(1)}, f32[8,512]{1,0:T(8,128)}, u32[]{:S(2)}) copy-start(f32[8,512]{1,0:T(8,128)} %get-tuple-element.12) | copy-start | bytes 49156
  240.0 311.4 %copy-start = (f32[8,32,512]{2,1,0:T(8,128)S(1)}, f32[8,32,512]{2,1,0:T(8,128)}, u32[]{:S(2)}) copy-start(f32[8,32,512]{2,1,0:T(8,128)} %param.13) | copy-start | bytes 1572868
  240.0 312.7 %copy-start.1 = (f32[8,32,512]{2,1,0:T(8,128)S(1)}, f32[8,32,512]{2,1,0:T(8,128)}, u32[]{:S(2)}) copy-start(f32[8,32,512]{2,1,0:T(8,128)} %param.11) | copy-start | bytes 1572868
  240.0 312.7 %copy-start.2 = (f32[8,32,512]{2,1,0:T(8,128)S(1)}, f32[8,32,512]{2,1,0:T(8,128)}, u32[]{:S(2)}) copy-start(f32[8,32,512]{2,1,0:T(8,128)} %param.12) | copy-start | bytes 1572868
  240.0 422.3 %all-gather.13.cloned.1.call-start = ((), (), s32[]{:S(2)}) async-start(), calls=%async_computation.9 | async-start | bytes 4456448 | tf_op jit(solution)/shard_map/all_gather | solution.py:90
  272.6 344.1 %copy-start.3 = (f32[8,32,512]{2,0,1:T(8,128)S(1)}, f32[8,32,512]{2,0,1:T(8,128)}, u32[]{:S(2)}) copy-start(f32[8,32,512]{2,0,1:T(8,128)} %reduce-scatter.6.cloned.1.call-done) | copy-start | bytes 1572868
  614.4 99.2 %all-gather.17.cloned.1.call-start = ((), (), s32[]{:S(2)}) async-start(), calls=%async_computation.11 | async-start | bytes 4456448 | tf_op jit(solution)/shard_map/all_gather | solution.py:92
  616.4 148.5 %all-gather.15.cloned.1.call-start = ((), (), s32[]{:S(2)}) async-start(), calls=%async_computation.10 | async-start | bytes 4456448 | tf_op jit(solution)/shard_map/all_gather | solution.py:91
Sparse Core Ops, SparseCore 0:
  9.5 53.2 all-gather.10
  65.0 49.0 all-gather.6
  116.3 49.0 all-gather.8
  169.4 103.1 reduce-scatter.5
  276.5 104.4 reduce-scatter.7
  384.9 104.4 reduce-scatter.3
  614.5 47.7 all-gather.12
  664.5 49.0 all-gather.16
  715.8 49.0 all-gather.14
where the time goes:
time: 795 us; the launch traced here: 794 us
  waiting for transfers between devices  472 us (59%)
  matrix products  147 us (18%)
  blocking collectives  118 us (15%)
  local copies, waits for them, and re-layouts  21.1 us (3%)
  other arithmetic  20.9 us (3%)
  between operations  13.3 us (2%)
    reduce_scatter x1, waiting for transfers between devices, on_device(): lax.psum_scatter(grad_gate, ('seq', 'sub'), scatter_dimension=1, tiled=True)  107 us
    reduce_scatter x1, waiting for transfers between devices, on_device(): lax.psum_scatter(grad_down, ('seq', 'sub'), scatter_dimension=1, tiled=True)  107 us
    psum x1, blocking collectives, on_device(): lax.psum((column_squares(fast_gate), column_squares(fast_up), column_squa...  60.4 us
    psum x1, blocking collectives, on_device(): lax.psum((column_squares(moved_all[0]), column_squares(moved_all[1]), col...  57.7 us
    all_gather x1, waiting for transfers between devices, on_device(): lax.all_gather(renewed[1], ('seq', 'sub'), axis=1, tiled=True)  51.2 us
    all_gather x1, waiting for transfers between devices, on_device(): lax.all_gather(fast_gate.astype(jnp.bfloat16), ('seq', 'sub'), axis=1, ti...  47.5 us
    all_gather x1, waiting for transfers between devices, on_device(): lax.all_gather(renewed[0], ('seq', 'sub'), axis=1, tiled=True)  44.6 us
    all_gather x1, waiting for transfers between devices, on_device(): lax.all_gather(fast_down.astype(jnp.bfloat16), ('seq', 'sub'), axis=1, ti...  36.5 us
  transfers between devices with their start and end apart: 9, of which 9 were waited for; matrix products, arithmetic and copies ran while one was open for 20% of the time, Pallas kernels for 0%

commit v1 on v0

--- a/solution.py
+++ b/solution.py
@@ -5,6 +5,27 @@
 
 EPSILON = 1e-06
 STEP_SIZE = 0.5
+
+
+def collect(x, axis, dim):
+    size, place, rows = (lax.axis_size(axis), lax.axis_index(axis), x.shape[dim])
+    right = [(i, (i + 1) % size) for i in range(size)]
+    left = [(i, (i - 1) % size) for i in range(size)]
+    whole = jnp.zeros((*x.shape[:dim], size * rows, *x.shape[dim + 1 :]), x.dtype)
+    whole = lax.dynamic_update_slice_in_dim(whole, x, place * rows, axis=dim)
+    from_left = from_right = x
+    middle = size // 2
+    for step in range(1, middle + 1):
+        from_left = lax.ppermute(from_left, axis, right)
+        whole = lax.dynamic_update_slice_in_dim(
+            whole, from_left, (place - step) % size * rows, axis=dim
+        )
+        if step < size - middle:
+            from_right = lax.ppermute(from_right, axis, left)
+            whole = lax.dynamic_update_slice_in_dim(
+                whole, from_right, (place + step) % size * rows, axis=dim
+            )
+    return whole
 
 
 def column_squares(matrix):
@@ -89,7 +110,7 @@
     new_gate, new_up, new_down = (
         lax.all_gather(renewed[0], ("seq", "sub"), axis=1, tiled=True),
         lax.all_gather(renewed[1], ("seq", "sub"), axis=1, tiled=True),
-        lax.all_gather(renewed[2], ("seq", "sub"), axis=1, tiled=True),
+        collect(renewed[2], ("seq", "sub"), 1),
     )
     return apply_fast(queries, new_gate, new_up, new_down)
 

time: 795 us -> 760 us (0.956)
  waiting for transfers between devices: 472 us -> 392 us
  starting transfers between devices: 0.74 us -> 32.2 us
  local copies, waits for them, and re-layouts: 21.1 us -> 34.8 us
    all_gather x1, waiting for transfers between devices: 44.6 us -> 0.01 us  [on_device(): lax.all_gather(renewed[0], ('seq', 'sub'), axis=1, tiled=True)]
    ppermute x0 -> x15, waiting for transfers between devices: none -> 41.4 us  [the longest x8 30.8 us: collect(): from_left = lax.ppermute(from_left, axis, right)]
    all_gather x1, waiting for transfers between devices: 51.2 us -> 10.8 us  [on_device(): lax.all_gather(renewed[1], ('seq', 'sub'), axis=1, tiled=True)]
    all_gather x1 -> x0, waiting for transfers between devices: 36.4 us -> none  [on_device(): lax.all_gather(renewed[2], ('seq', 'sub'), axis=1, tiled=True)]
    ppermute x0 -> x15, starting transfers between devices: none -> 31.7 us  [the longest x7 31.7 us: collect(): from_right = lax.ppermute(from_right, axis, left)]
    dynamic_update_slice x0 -> x15, local copies, waits for them, and re-layouts: none -> 11.4 us  [the longest x8 6.01 us: collect(): lax.dynamic_update_slice_in_dim(whole, from_left, (place - step) % size *...]
  transfers between devices with their start and end apart: 9 -> 23, of which waited for: 9 -> 19; matrix products, arithmetic and copies ran while one was open for 20% -> 22% of each run, Pallas kernels for 0% -> 0%
where the time goes in v1:
time: 760 us; the launch traced here: 759 us
  waiting for transfers between devices  392 us (52%)
  matrix products  148 us (19%)
  blocking collectives  118 us (16%)
  local copies, waits for them, and re-layouts  34.8 us (5%)
  starting transfers between devices  32.2 us (4%)
  other arithmetic  20.3 us (3%)
  between operations  13.7 us (2%)
    reduce_scatter x1, waiting for transfers between devices, on_device(): lax.psum_scatter(grad_down, ('seq', 'sub'), scatter_dimension=1, tiled=True)  107 us
    reduce_scatter x1, waiting for transfers between devices, on_device(): lax.psum_scatter(grad_gate, ('seq', 'sub'), scatter_dimension=1, tiled=True)  107 us
    psum x1, blocking collectives, on_device(): lax.psum((column_squares(fast_gate), column_squares(fast_up), column_squa...  60.4 us
    psum x1, blocking collectives, on_device(): lax.psum((column_squares(moved_all[0]), column_squares(moved_all[1]), col...  57.7 us
    all_gather x1, waiting for transfers between devices, on_device(): lax.all_gather(fast_gate.astype(jnp.bfloat16), ('seq', 'sub'), axis=1, ti...  47.5 us
    all_gather x1, waiting for transfers between devices, on_device(): lax.all_gather(fast_down.astype(jnp.bfloat16), ('seq', 'sub'), axis=1, ti...  36.5 us
    reduce_scatter x1, waiting for transfers between devices, on_device(): lax.psum_scatter(grad_up, ('seq', 'sub'), scatter_dimension=1, tiled=True)  32.6 us
    ppermute x7, starting transfers between devices, collect(): from_right = lax.ppermute(from_right, axis, left)  31.7 us
  transfers between devices with their start and end apart: 23, of which 19 were waited for; matrix products, arithmetic and copies ran while one was open for 22% of the time, Pallas kernels for 0%

profile of v1, /device:TPU:0, one launch (start us, length us, event | category | flops | bytes accessed | tf_op | source)
XLA Modules:
  0.0 759.2 jit_solution(16999665065831587419)
XLA Ops:
  6.5 2.6 multiply_reduce_fusion.8
  9.2 2.6 multiply_reduce_fusion.1
  11.8 2.7 multiply_reduce_fusion.3
  14.6 0.8 multiply_negate_fusion
  15.3 47.5 %all-gather.10.cloned.1.call-done = bf16[8,512,512]{2,1,0:T(8,128)(2,1)} async-done(((bf16[8,32,512]{2,1,0:T(8,128)(2,1)}), bf16[8,512,512]{2,1,0:T(8,128)(2,1)}) %all-gather.10.cloned.1.call-update) | async-done | bytes 4194320 | tf_op jit(solution)/shard_map/all_gather | solution.py:74
  62.9 14.8 %fusion.19 = f32[8,1024,512]{2,1,0:T(8,128)} fusion(bf16[8,1024,512]{2,1,0:T(8,128)(2,1)} %param.8, bf16[8,512,512]{2,1,0:T(8,128)(2,1)} %all-gather.10.cloned.1.call-done), kind=kOutput, calls=%fused_computation.66 | convolution fusion | flops 4294967296 | bytes 29360128 | tf_op jit(solution)/shard_map/htd,hdf->htf/dot_general | solution.py:55
  77.7 36.5 %all-gather.6.cloned.1.call-done = bf16[8,512,512]{2,1,0:T(8,128)(2,1)} async-done(((bf16[8,32,512]{2,1,0:T(8,128)(2,1)}), bf16[8,512,512]{2,1,0:T(8,128)(2,1)}) %all-gather.6.cloned.1.call-update) | async-done | bytes 4194320 | tf_op jit(solution)/shard_map/all_gather | solution.py:76
  114.1 11.7 %fusion.7 = f32[8,1024,512]{2,1,0:T(8,128)} fusion(bf16[8,512,512]{2,1,0:T(8,128)(2,1)} %all-gather.6.cloned.1.call-done, bf16[8,1024,512]{2,1,0:T(8,128)(2,1)} %param.9, f32[8,1024]{1,0:T(8,128)S(1)} %multiply_negate_fusion), kind=kOutput, calls=%fused_computation.15 | convolution fusion | flops 4307550208 | bytes 29392896 | tf_op jit(solution)/shard_map/htd,hfd->htf/dot_general | solution.py:59
  125.8 19.5 %fusion.13 = f32[8,512,512]{1,2,0:T(8,128)} fusion(bf16[8,1024,512]{2,1,0:T(8,128)(2,1)} %param.8, f32[8,1024,512]{2,1,0:T(8,128)} %fusion.7, f32[8,1024,512]{2,1,0:T(8,128)} %fusion.19), kind=kOutput, calls=%fused_computation.21 | convolution fusion | flops 4320133120 | bytes 50331648 | tf_op jit(solution)/shard_map/htd,htf->hdf/dot_general | solution.py:65
  145.3 10.5 %copy.18 = f32[8,512,512]{2,0,1:T(8,128)} copy(f32[8,512,512]{1,2,0:T(8,128)} %fusion.13) | data formatting | bytes 16777216 | tf_op jit(solution)/shard_map/htd,htf->hdf/dot_general | solution.py:65
  156.0 9.4 %all-gather.8.cloned.1.call-done = bf16[8,512,512]{2,1,0:T(8,128)(2,1)} async-done(((bf16[8,32,512]{2,1,0:T(8,128)(2,1)}), bf16[8,512,512]{2,1,0:T(8,128)(2,1)}) %all-gather.8.cloned.1.call-update) | async-done | bytes 4194320 | tf_op jit(solution)/shard_map/all_gather | solution.py:75
  165.4 16.6 %fusion.18 = f32[8,1024,512]{2,1,0:T(8,128)} fusion(bf16[8,1024,512]{2,1,0:T(8,128)(2,1)} %param.8, bf16[8,512,512]{2,1,0:T(8,128)(2,1)} %all-gather.8.cloned.1.call-done), kind=kOutput, calls=%fused_computation.65 | convolution fusion | flops 4294967296 | bytes 29360128 | tf_op jit(solution)/shard_map/htd,hdf->htf/dot_general | solution.py:56
  182.0 21.8 %fusion.5 = f32[8,512,512]{2,1,0:T(8,128)} fusion(f32[8,1024,512]{2,1,0:T(8,128)} %fusion.18, f32[8,1024,512]{2,1,0:T(8,128)} %fusion.19, bf16[8,1024,512]{2,1,0:T(8,128)(2,1)} %param.9, f32[8,1024]{1,0:T(8,128)S(1)} %multiply_negate_fusion), kind=kOutput, calls=%fused_computation.13 | convolution fusion | flops 4332716032 | bytes 50364416 | tf_op jit(solution)/shard_map/htf,htd->hfd/dot_general | solution.py:66
  203.9 25.5 %fusion.12 = f32[8,512,512]{1,2,0:T(8,128)} fusion(bf16[8,1024,512]{2,1,0:T(8,128)(2,1)} %param.8, f32[8,1024,512]{2,1,0:T(8,128)} %fusion.19, f32[8,1024,512]{2,1,0:T(8,128)} %fusion.7, f32[8,1024,512]{2,1,0:T(8,128)} %fusion.18), kind=kOutput, calls=%fused_computation.20 | convolution fusion | flops 4336910336 | bytes 67108864 | tf_op jit(solution)/shard_map/htd,htf->hdf/dot_general | solution.py:64
  229.4 10.6 %copy.16 = f32[8,512,512]{2,0,1:T(8,128)} copy(f32[8,512,512]{1,2,0:T(8,128)} %fusion.12) | data formatting | bytes 16777216 | tf_op jit(solution)/shard_map/htd,htf->hdf/dot_general | solution.py:64
  240.0 32.6 %reduce-scatter.6.cloned.1.call-done = f32[8,32,512]{2,0,1:T(8,128)} async-done(((f32[8,512,512]{2,0,1:T(8,128)}), f32[8,32,512]{2,0,1:T(8,128)}) %reduce-scatter.6.cloned.1.call-update) | async-done | bytes 524304 | tf_op jit(solution)/shard_map/reduce_scatter | solution.py:81
  272.6 1.3 multiply_reduce_fusion.6
  273.9 107.1 %reduce-scatter.8.cloned.1.call-done = f32[8,32,512]{2,1,0:T(8,128)} async-done(((f32[8,512,512]{2,1,0:T(8,128)}), f32[8,32,512]{2,1,0:T(8,128)}) %reduce-scatter.8.cloned.1.call-update) | async-done | bytes 524304 | tf_op jit(solution)/shard_map/reduce_scatter | solution.py:82
  381.0 1.3 multiply_reduce_fusion.5
  382.3 107.0 %reduce-scatter.4.cloned.1.call-done = f32[8,32,512]{2,0,1:T(8,128)} async-done(((f32[8,512,512]{2,0,1:T(8,128)}), f32[8,32,512]{2,0,1:T(8,128)}) %reduce-scatter.4.cloned.1.call-update) | async-done | bytes 524304 | tf_op jit(solution)/shard_map/reduce_scatter | solution.py:80
  489.3 1.3 multiply_reduce_fusion.7
  490.6 60.4 %all-reduce.1 = (f32[8,3]{0,1:T(4,128)S(1)}, f32[8,512]{1,0:T(8,128)S(1)}, f32[8,512]{1,0:T(8,128)S(1)}, f32[8,512]{1,0:T(8,128)S(1)}) all-reduce(f32[8,3]{0,1:T(4,128)S(1)} %pad_maximum_fusion, f32[8,512]{1,0:T(8,128)S(1)} %copy-done.6, ...), channel_id=1, replica_groups=mesh['groups'=2,'seq'=8,'head'=1,'sub'=2] {'seq','sub'}, use_global_device_ids=true, to_apply=%region_9.0 | all-reduce | flops 12312 | bytes 98496 | tf_op jit(solution)/shard_map/psum | solution.py:93
  551.4 1.2 multiply_reduce_fusion
  552.6 1.9 multiply_reduce_fusion.2
  554.5 57.7 %all-reduce = (f32[8,512]{1,0:T(8,128)S(1)}, f32[8,512]{1,0:T(8,128)S(1)}, f32[8,512]{1,0:T(8,128)S(1)}) all-reduce(f32[8,512]{1,0:T(8,128)S(1)} %multiply_reduce_fusion, f32[8,512]{1,0:T(8,128)S(1)} %get-tuple-element.24, f32[8,512]{1,0:T(8,128)S(1)} %get-tuple-element.23), channel_id=1, replica_groups=mesh['groups'=2,'seq'=8,'head'=1,'sub'=2] {'seq','sub'}, use_global_device_ids=true, to_apply=%region_21.0 | all-reduce | flops 12288 | bytes 98304 | tf_op jit(solution)/shard_map/psum | solution.py:102
  612.3 2.1 multiply_convert_fusion.15
  614.4 2.1 multiply_convert_fusion.14
  616.6 0.4 broadcast_in_dim.2
  617.1 1.9 copy-done.4
  619.0 4.4 collective-permute-start.1
  623.5 8.6 %collective-permute-done = bf16[8,32,512]{2,1,0:T(8,128)(2,1)S(1)} collective-permute-done((bf16[8,32,512]{2,1,0:T(8,128)(2,1)S(1)}, bf16[8,32,512]{2,1,0:T(8,128)(2,1)S(1)}, u32[]{:S(2)}, u32[]{:S(2)}) %collective-permute-start) | collective-permute-done | bytes 262176 | tf_op jit(solution)/shard_map/ppermute | solution.py:19
  632.1 4.4 collective-permute-start.3
  636.5 4.2 collective-permute-done.2
  640.7 4.4 collective-permute-start.5
  645.1 9.3 %collective-permute-done.4 = bf16[8,32,512]{2,1,0:T(8,128)(2,1)S(1)} collective-permute-done((bf16[8,32,512]{2,1,0:T(8,128)(2,1)S(1)}, bf16[8,32,512]{2,1,0:T(8,128)(2,1)S(1)}, u32[]{:S(2)}, u32[]{:S(2)}) %collective-permute-start.4) | collective-permute-done | bytes 262176 | tf_op jit(solution)/shard_map/ppermute | solution.py:19
  654.4 0.7 constant_dynamic-update-slice_fusion.14
  655.2 4.5 collective-permute-start.7
  659.6 0.7 constant_dynamic-update-slice_fusion.13
  660.4 4.1 collective-permute-done.6
  664.5 0.8 constant_dynamic-update-slice_fusion.12
  665.3 0.7 constant_dynamic-update-slice_fusion.11
  666.0 2.6 collective-permute-done.7
  668.6 4.6 collective-permute-start.9
  673.2 0.7 constant_dynamic-update-slice_fusion.10
  674.2 0.8 constant_dynamic-update-slice_fusion.9
  675.0 0.8 constant_dynamic-update-slice_fusion.8
  675.7 1.3 collective-permute-done.9
  677.1 4.7 collective-permute-start.11
  681.8 0.8 constant_dynamic-update-slice_fusion.7
  682.7 0.8 constant_dynamic-update-slice_fusion.6
  683.4 0.8 constant_dynamic-update-slice_fusion.5
  684.2 1.8 collective-permute-done.11
  686.1 4.6 collective-permute-start.13
  690.7 0.7 constant_dynamic-update-slice_fusion.4
  691.4 1.3 collective-permute-done.12
  692.7 0.8 constant_dynamic-update-slice_fusion.3
  693.5 0.8 constant_dynamic-update-slice_fusion.2
  694.2 4.8 collective-permute-done.13
  699.1 0.8 constant_dynamic-update-slice_fusion.1
  699.8 3.0 collective-permute-done.14
  702.8 0.7 constant_dynamic-update-slice_fusion
  703.6 15.5 %fusion.10 = f32[8,512,1024]{1,2,0:T(8,128)} fusion(bf16[8,1024,512]{2,1,0:T(8,128)(2,1)} %param.7, bf16[8,512,512]{2,0,1:T(8,128)(2,1)} %all-gather.12.cloned.1.call-done), kind=kOutput, calls=%fused_computation.18 | convolution fusion | flops 4294967296 | bytes 29360128 | tf_op jit(solution)/shard_map/htd,hdf->htf/dot_general | solution.py:46
  719.0 10.8 %all-gather.14.cloned.1.call-done = bf16[8,512,512]{2,0,1:T(8,128)(2,1)} async-done(((bf16[8,32,512]{2,0,1:T(8,128)(2,1)}), bf16[8,512,512]{2,0,1:T(8,128)(2,1)}) %all-gather.14.cloned.1.call-update) | async-done | bytes 4194320 | tf_op jit(solution)/shard_map/all_gather | solution.py:112
  729.8 22.5 %convolution_convert_fusion = bf16[8,1024,512]{2,1,0:T(8,128)(2,1)} fusion(bf16[8,512,512]{2,1,0:T(8,128)(2,1)} %constant_dynamic-update-slice_fusion, f32[8,512,1024]{1,2,0:T(8,128)} %fusion.10, bf16[8,1024,512]{2,1,0:T(8,128)(2,1)} %param.7, bf16[8,512,512]{2,0,1:T(8,128)(2,1)} %all-gather.14.cloned.1.call-done), kind=kOutput, calls=%fused_computation.16 | convolution fusion | flops 8619294720 | bytes 41943040 | tf_op jit(solution)/shard_map/htf,hfd->htd/dot_general | solution.py:49
  (54 shorter events, 1.6 us)
Async XLA Ops:
  6.5 56.3 %all-gather.10.cloned.1.call-start = ((), (), s32[]{:S(2)}) async-start(), calls=%async_computation.5 | async-start | bytes 4456448 | tf_op jit(solution)/shard_map/all_gather | solution.py:74
  9.1 105.0 %all-gather.6.cloned.1.call-start = ((), (), s32[]{:S(2)}) async-start(), calls=%async_computation.3 | async-start | bytes 4456448 | tf_op jit(solution)/shard_map/all_gather | solution.py:76
  11.8 153.7 %all-gather.8.cloned.1.call-start = ((), (), s32[]{:S(2)}) async-start(), calls=%async_computation.4 | async-start | bytes 4456448 | tf_op jit(solution)/shard_map/all_gather | solution.py:75
  14.5 258.1 %reduce-scatter.6.cloned.1.call-start = ((), (), s32[]{:S(2)}) async-start(), calls=%async_computation.7 | async-start | bytes 8912896 | tf_op jit(solution)/shard_map/reduce_scatter | solution.py:81
  155.8 225.2 %reduce-scatter.8.cloned.1.call-start = ((), (), s32[]{:S(2)}) async-start(), calls=%async_computation.8 | async-start | bytes 8912896 | tf_op jit(solution)/shard_map/reduce_scatter | solution.py:82
  203.8 285.5 %reduce-scatter.4.cloned.1.call-start = ((), (), s32[]{:S(2)}) async-start(), calls=%async_computation.6 | async-start | bytes 8912896 | tf_op jit(solution)/shard_map/reduce_scatter | solution.py:80
  239.9 250.7 %copy-start.5 = (f32[8,512]{1,0:T(8,128)S(1)}, f32[8,512]{1,0:T(8,128)}, u32[]{:S(2)}) copy-start(f32[8,512]{1,0:T(8,128)} %get-tuple-element.16) | copy-start | bytes 49156
  239.9 250.7 %copy-start.6 = (f32[8,512]{1,0:T(8,128)S(1)}, f32[8,512]{1,0:T(8,128)}, u32[]{:S(2)}) copy-start(f32[8,512]{1,0:T(8,128)} %get-tuple-element.18) | copy-start | bytes 49156
  239.9 250.7 %copy-start.7 = (f32[8,512]{1,0:T(8,128)S(1)}, f32[8,512]{1,0:T(8,128)}, u32[]{:S(2)}) copy-start(f32[8,512]{1,0:T(8,128)} %get-tuple-element.14) | copy-start | bytes 49156
  239.9 311.4 %copy-start.2 = (f32[8,32,512]{2,1,0:T(8,128)S(1)}, f32[8,32,512]{2,1,0:T(8,128)}, u32[]{:S(2)}) copy-start(f32[8,32,512]{2,1,0:T(8,128)} %param.13) | copy-start | bytes 1572868
  239.9 312.7 %copy-start = (f32[8,32,512]{2,1,0:T(8,128)S(1)}, f32[8,32,512]{2,1,0:T(8,128)}, u32[]{:S(2)}) copy-start(f32[8,32,512]{2,1,0:T(8,128)} %param.11) | copy-start | bytes 1572868
  240.0 312.7 %copy-start.1 = (f32[8,32,512]{2,1,0:T(8,128)S(1)}, f32[8,32,512]{2,1,0:T(8,128)}, u32[]{:S(2)}) copy-start(f32[8,32,512]{2,1,0:T(8,128)} %param.12) | copy-start | bytes 1572868
  240.0 463.6 %all-gather.12.cloned.1.call-start = ((), (), s32[]{:S(2)}) async-start(), calls=%async_computation.9 | async-start | bytes 4456448 | tf_op jit(solution)/shard_map/all_gather | solution.py:111
  381.0 236.0 %copy-start.3 = (f32[8,32,512]{2,1,0:T(8,128)S(1)}, f32[8,32,512]{2,1,0:T(8,128)}, u32[]{:S(2)}) copy-start(f32[8,32,512]{2,1,0:T(8,128)} %reduce-scatter.8.cloned.1.call-done) | copy-start | bytes 1572868
  614.4 115.5 %all-gather.14.cloned.1.call-start = ((), (), s32[]{:S(2)}) async-start(), calls=%async_computation.10 | async-start | bytes 4456448 | tf_op jit(solution)/shard_map/all_gather | solution.py:112
  617.1 1.9 copy-start.4
  619.0 13.0 %collective-permute-start = (bf16[8,32,512]{2,1,0:T(8,128)(2,1)S(1)}, bf16[8,32,512]{2,1,0:T(8,128)(2,1)S(1)}, u32[]{:S(2)}, u32[]{:S(2)}) collective-permute-start(bf16[8,32,512]{2,1,0:T(8,128)(2,1)S(1)} %get-tuple-element.13), channel_id=1, source_target_pairs={{0,1},{1,2},{2,3},{3,4},{4,5},{5,6},{6,7},{7,8},{8,9},{9,10},{10,1... | collective-permute-start | bytes 786440 | tf_op jit(solution)/shard_map/ppermute | solution.py:19
  619.0 13.0 %collective-permute-start.1 = (bf16[8,32,512]{2,1,0:T(8,128)(2,1)S(1)}, bf16[8,32,512]{2,1,0:T(8,128)(2,1)S(1)}, u32[]{:S(2)}, u32[]{:S(2)}) collective-permute-start(bf16[8,32,512]{2,1,0:T(8,128)(2,1)S(1)} %get-tuple-element.13), channel_id=1, source_target_pairs={{0,15},{1,0},{2,1},{3,2},{4,3},{5,4},{6,5},{7,6},{8,7},{9,8},{10,9... | collective-permute-start | bytes 786440 | tf_op jit(solution)/shard_map/ppermute | solution.py:24
  632.1 8.6 %collective-permute-start.2 = (bf16[8,32,512]{2,1,0:T(8,128)(2,1)S(1)}, bf16[8,32,512]{2,1,0:T(8,128)(2,1)S(1)}, u32[]{:S(2)}, u32[]{:S(2)}) collective-permute-start(bf16[8,32,512]{2,1,0:T(8,128)(2,1)S(1)} %collective-permute-done), channel_id=1, source_target_pairs={{0,1},{1,2},{2,3},{3,4},{4,5},{5,6},{6,7},{7,8},{8,9},{9,10},{10,1... | collective-permute-start | bytes 786440 | tf_op jit(solution)/shard_map/ppermute | solution.py:19
  632.1 8.6 %collective-permute-start.3 = (bf16[8,32,512]{2,1,0:T(8,128)(2,1)S(1)}, bf16[8,32,512]{2,1,0:T(8,128)(2,1)S(1)}, u32[]{:S(2)}, u32[]{:S(2)}) collective-permute-start(bf16[8,32,512]{2,1,0:T(8,128)(2,1)S(1)} %collective-permute-done.1), channel_id=1, source_target_pairs={{0,15},{1,0},{2,1},{3,2},{4,3},{5,4},{6,5},{7,6},{8,7},{9,8},{10,9... | collective-permute-start | bytes 786440 | tf_op jit(solution)/shard_map/ppermute | solution.py:24
  640.7 13.8 %collective-permute-start.4 = (bf16[8,32,512]{2,1,0:T(8,128)(2,1)S(1)}, bf16[8,32,512]{2,1,0:T(8,128)(2,1)S(1)}, u32[]{:S(2)}, u32[]{:S(2)}) collective-permute-start(bf16[8,32,512]{2,1,0:T(8,128)(2,1)S(1)} %collective-permute-done.2), channel_id=1, source_target_pairs={{0,1},{1,2},{2,3},{3,4},{4,5},{5,6},{6,7},{7,8},{8,9},{9,10},{10,1... | collective-permute-start | bytes 786440 | tf_op jit(solution)/shard_map/ppermute | solution.py:19
  640.7 14.5 %collective-permute-start.5 = (bf16[8,32,512]{2,1,0:T(8,128)(2,1)S(1)}, bf16[8,32,512]{2,1,0:T(8,128)(2,1)S(1)}, u32[]{:S(2)}, u32[]{:S(2)}) collective-permute-start(bf16[8,32,512]{2,1,0:T(8,128)(2,1)S(1)} %collective-permute-done.3), channel_id=1, source_target_pairs={{0,15},{1,0},{2,1},{3,2},{4,3},{5,4},{6,5},{7,6},{8,7},{9,8},{10,9... | collective-permute-start | bytes 786440 | tf_op jit(solution)/shard_map/ppermute | solution.py:24
  654.4 10.1 %collective-permute-start.6 = (bf16[8,32,512]{2,1,0:T(8,128)(2,1)S(1)}, bf16[8,32,512]{2,1,0:T(8,128)(2,1)S(1)}, u32[]{:S(2)}, u32[]{:S(2)}) collective-permute-start(bf16[8,32,512]{2,1,0:T(8,128)(2,1)S(1)} %collective-permute-done.4), channel_id=1, source_target_pairs={{0,1},{1,2},{2,3},{3,4},{4,5},{5,6},{6,7},{7,8},{8,9},{9,10},{10,1... | collective-permute-start | bytes 786440 | tf_op jit(solution)/shard_map/ppermute | solution.py:19
  655.2 13.4 %collective-permute-start.7 = (bf16[8,32,512]{2,1,0:T(8,128)(2,1)S(1)}, bf16[8,32,512]{2,1,0:T(8,128)(2,1)S(1)}, u32[]{:S(2)}, u32[]{:S(2)}) collective-permute-start(bf16[8,32,512]{2,1,0:T(8,128)(2,1)S(1)} %collective-permute-done.5), channel_id=1, source_target_pairs={{0,15},{1,0},{2,1},{3,2},{4,3},{5,4},{6,5},{7,6},{8,7},{9,8},{10,9... | collective-permute-start | bytes 786440 | tf_op jit(solution)/shard_map/ppermute | solution.py:24
  664.5 9.7 %collective-permute-start.8 = (bf16[8,32,512]{2,1,0:T(8,128)(2,1)S(1)}, bf16[8,32,512]{2,1,0:T(8,128)(2,1)S(1)}, u32[]{:S(2)}, u32[]{:S(2)}) collective-permute-start(bf16[8,32,512]{2,1,0:T(8,128)(2,1)S(1)} %collective-permute-done.6), channel_id=1, source_target_pairs={{0,1},{1,2},{2,3},{3,4},{4,5},{5,6},{6,7},{7,8},{8,9},{9,10},{10,1... | collective-permute-start | bytes 786440 | tf_op jit(solution)/shard_map/ppermute | solution.py:19
  668.6 8.5 %collective-permute-start.9 = (bf16[8,32,512]{2,1,0:T(8,128)(2,1)S(1)}, bf16[8,32,512]{2,1,0:T(8,128)(2,1)S(1)}, u32[]{:S(2)}, u32[]{:S(2)}) collective-permute-start(bf16[8,32,512]{2,1,0:T(8,128)(2,1)S(1)} %collective-permute-done.7), channel_id=1, source_target_pairs={{0,15},{1,0},{2,1},{3,2},{4,3},{5,4},{6,5},{7,6},{8,7},{9,8},{10,9... | collective-permute-start | bytes 786440 | tf_op jit(solution)/shard_map/ppermute | solution.py:24
  674.2 8.5 %collective-permute-start.10 = (bf16[8,32,512]{2,1,0:T(8,128)(2,1)S(1)}, bf16[8,32,512]{2,1,0:T(8,128)(2,1)S(1)}, u32[]{:S(2)}, u32[]{:S(2)}) collective-permute-start(bf16[8,32,512]{2,1,0:T(8,128)(2,1)S(1)} %collective-permute-done.8), channel_id=1, source_target_pairs={{0,1},{1,2},{2,3},{3,4},{4,5},{5,6},{6,7},{7,8},{8,9},{9,10},{10,1... | collective-permute-start | bytes 786440 | tf_op jit(solution)/shard_map/ppermute | solution.py:19
  677.1 9.0 %collective-permute-start.11 = (bf16[8,32,512]{2,1,0:T(8,128)(2,1)S(1)}, bf16[8,32,512]{2,1,0:T(8,128)(2,1)S(1)}, u32[]{:S(2)}, u32[]{:S(2)}) collective-permute-start(bf16[8,32,512]{2,1,0:T(8,128)(2,1)S(1)} %collective-permute-done.9), channel_id=1, source_target_pairs={{0,15},{1,0},{2,1},{3,2},{4,3},{5,4},{6,5},{7,6},{8,7},{9,8},{10,9... | collective-permute-start | bytes 786440 | tf_op jit(solution)/shard_map/ppermute | solution.py:24
  682.7 10.0 %collective-permute-start.12 = (bf16[8,32,512]{2,1,0:T(8,128)(2,1)S(1)}, bf16[8,32,512]{2,1,0:T(8,128)(2,1)S(1)}, u32[]{:S(2)}, u32[]{:S(2)}) collective-permute-start(bf16[8,32,512]{2,1,0:T(8,128)(2,1)S(1)} %collective-permute-done.10), channel_id=1, source_target_pairs={{0,1},{1,2},{2,3},{3,4},{4,5},{5,6},{6,7},{7,8},{8,9},{9,10},{10,1... | collective-permute-start | bytes 786440 | tf_op jit(solution)/shard_map/ppermute | solution.py:19
  686.1 13.0 %collective-permute-start.13 = (bf16[8,32,512]{2,1,0:T(8,128)(2,1)S(1)}, bf16[8,32,512]{2,1,0:T(8,128)(2,1)S(1)}, u32[]{:S(2)}, u32[]{:S(2)}) collective-permute-start(bf16[8,32,512]{2,1,0:T(8,128)(2,1)S(1)} %collective-permute-done.11), channel_id=1, source_target_pairs={{0,15},{1,0},{2,1},{3,2},{4,3},{5,4},{6,5},{7,6},{8,7},{9,8},{10,9... | collective-permute-start | bytes 786440 | tf_op jit(solution)/shard_map/ppermute | solution.py:24
  692.7 10.2 %collective-permute-start.14 = (bf16[8,32,512]{2,1,0:T(8,128)(2,1)S(1)}, bf16[8,32,512]{2,1,0:T(8,128)(2,1)S(1)}, u32[]{:S(2)}, u32[]{:S(2)}) collective-permute-start(bf16[8,32,512]{2,1,0:T(8,128)(2,1)S(1)} %collective-permute-done.12), channel_id=1, source_target_pairs={{0,1},{1,2},{2,3},{3,4},{4,5},{5,6},{6,7},{7,8},{8,9},{9,10},{10,1... | collective-permute-start | bytes 786440 | tf_op jit(solution)/shard_map/ppermute | solution.py:19
Sparse Core Ops, SparseCore 0:
  9.5 53.2 all-gather.9
  65.0 49.0 all-gather.5
  116.3 49.0 all-gather.7
  169.4 103.1 reduce-scatter.5
  276.5 104.4 reduce-scatter.7
  384.9 104.3 reduce-scatter.3
  614.5 58.8 all-gather.11
  675.5 54.2 all-gather.13
